TPU v7x, 32 devices: a whole 2x2x4 slice. The times are simulated.
32 devices in a mesh: dp: 8 (over z, x), tensor: 4 (over y, core).
Axes of the slice: x: 2, y: 2, z: 4, core: 2. Of those that a mesh axis runs over, the one named last changes fastest.
Arguments:
- layer_input: float32 [8, 1024, 768], P('dp', 'tensor'), may hold values from -40 to 40
- out_cotangent: float32 [8, 1024, 768], P('dp', 'tensor'), may hold values from -6 to 6
- mix_gain: bfloat16 [768], P('dp'), may hold values from 0.099609375 to 1.8984375
- mix_shift: bfloat16 [768], P('dp'), may hold values from -4 to 4
- query_weight: bfloat16 [768, 768], P('dp', 'tensor'), may hold values from -2 to 2
- query_bias: bfloat16 [64, 12], P('dp', 'tensor'), may hold values from -3 to 3
- key_weight: bfloat16 [768, 768], P('dp', 'tensor'), may hold values from -2 to 2
- value_weight: bfloat16 [768, 768], P('dp', 'tensor'), may hold values from -0.21875 to 0.21875
- value_bias: bfloat16 [64, 12], P('dp', 'tensor'), may hold values from -0.59765625 to 0.59765625
- output_weight: bfloat16 [768, 768], P('dp', 'tensor'), may hold values from -1.75 to 1.75
- output_bias: bfloat16 [768], P('dp'), may hold values from -4 to 4
- feed_gain: bfloat16 [768], P('dp'), may hold values from 0.099609375 to 1.8984375
- feed_shift: bfloat16 [768], P('dp'), may hold values from -4 to 4
- inner_weight: bfloat16 [768, 3072], P('dp', 'tensor'), may hold values from -0.21875 to 0.21875
- inner_bias: bfloat16 [64, 48], P('dp', 'tensor'), may hold values from -3 to 3
- outer_weight: bfloat16 [768, 3072], P('dp', 'tensor'), may hold values from -0.3125 to 0.3125
- outer_bias: bfloat16 [768], P('dp'), may hold values from -4 to 4
Outputs:
- layer_output: float32 [8, 1024, 768], P('dp', 'tensor')
- input_grad: float32 [8, 1024, 768], P('dp', 'tensor')
- mix_gain_grad: float32 [768], P(('dp', 'tensor'))
- mix_shift_grad: float32 [768], P(('dp', 'tensor'))
- query_weight_grad: float32 [768, 768], P('dp', 'tensor')
- query_bias_grad: float32 [64, 12], P('dp', 'tensor')
- key_weight_grad: float32 [768, 768], P('dp', 'tensor')
- value_weight_grad: float32 [768, 768], P('dp', 'tensor')
- value_bias_grad: float32 [64, 12], P('dp', 'tensor')
- output_weight_grad: float32 [768, 768], P('dp', 'tensor')
- output_bias_grad: float32 [768], P(('dp', 'tensor'))
- feed_gain_grad: float32 [768], P(('dp', 'tensor'))
- feed_shift_grad: float32 [768], P(('dp', 'tensor'))
- inner_weight_grad: float32 [768, 3072], P('dp', 'tensor')
- inner_bias_grad: float32 [64, 48], P('dp', 'tensor')
- outer_weight_grad: float32 [768, 3072], P('dp', 'tensor')
- outer_bias_grad: float32 [768], P(('dp', 'tensor'))
All inputs are finite; a program needn't handle non-finite values.
Results may differ from a plain program's by a relative error of at most 0.02.
Values may be sent and summed in bfloat16 or wider, within the bound.
A program may use at most 128 MiB of HBM per device.

v0:
```python
import math
import jax
import jax.numpy as jnp
from jax import lax
from jax.sharding import PartitionSpec as P

HD = 64
EPS = 1e-05
ROOT_HALF = 0.7071067811865476
DENSITY_NORM = 0.3989422804014327


def layer_norm(block, gain, shift):
    row_mean = jnp.mean(block, axis=-1, keepdims=True)
    centred = block - row_mean
    rstd = lax.rsqrt(jnp.mean(centred * centred, axis=-1, keepdims=True) + EPS)
    normed = centred * rstd
    lowered = (normed * gain.astype(jnp.float32) + shift.astype(jnp.float32)).astype(jnp.bfloat16)
    return (normed, rstd, lowered)


def norm_backward(gradient, normed, rstd, gain):
    scaled = gradient * gain.astype(jnp.float32)
    first = jnp.mean(scaled, axis=-1, keepdims=True)
    second = jnp.mean(scaled * normed, axis=-1, keepdims=True)
    return (scaled - first - normed * second) * rstd


def gelu_value(preact):
    return 0.5 * preact * (1.0 + lax.erf(preact * ROOT_HALF))


def gelu_slope(preact):
    return 0.5 * (1.0 + lax.erf(preact * ROOT_HALF)) + preact * DENSITY_NORM * jnp.exp(
        -0.5 * preact * preact
    )


def matmul(left, right):
    return jnp.dot(left, right, preferred_element_type=jnp.float32)


def token_product(left, right):
    return lax.dot_general(
        left, right, (((0,), (0,)), ((), ())), preferred_element_type=jnp.float32
    )


def split_heads(block):
    return block.reshape(block.shape[0], block.shape[1] // HD, HD)


def attend(operands):
    queries, key_rows, values = operands
    score_scale = 1.0 / math.sqrt(HD)
    scores = (
        jnp.einsum(
            "qhd,khd->hqk",
            split_heads(queries),
            split_heads(key_rows),
            preferred_element_type=jnp.float32,
        )
        * score_scale
    )
    row_max = jnp.max(scores, axis=-1, keepdims=True)
    log_total = row_max + jnp.log(jnp.sum(jnp.exp(scores - row_max), axis=-1, keepdims=True))
    prob_low = jnp.exp(scores - log_total).astype(jnp.bfloat16)
    context = jnp.einsum(
        "hqk,khd->qhd", prob_low, split_heads(values), preferred_element_type=jnp.float32
    )
    return (context.reshape(queries.shape).astype(jnp.bfloat16), log_total)


def attend_back(operands):
    queries, key_rows, values, context_grad, log_total = operands
    score_scale = 1.0 / math.sqrt(HD)
    query_heads = split_heads(queries)
    key_heads = split_heads(key_rows)
    grad_heads = split_heads(context_grad)
    scores = (
        jnp.einsum("qhd,khd->hqk", query_heads, key_heads, preferred_element_type=jnp.float32)
        * score_scale
    )
    prob_full = jnp.exp(scores - log_total)
    prob_low = prob_full.astype(jnp.bfloat16)
    value_grad = jnp.einsum(
        "hqk,qhd->khd", prob_low, grad_heads, preferred_element_type=jnp.float32
    )
    prob_grad = jnp.einsum(
        "qhd,khd->hqk", grad_heads, split_heads(values), preferred_element_type=jnp.float32
    )
    row_dot = jnp.sum(prob_full * prob_grad, axis=-1, keepdims=True)
    score_grad = (prob_full * (prob_grad - row_dot) * score_scale).astype(jnp.bfloat16)
    query_grad = jnp.einsum(
        "hqk,khd->qhd", score_grad, key_heads, preferred_element_type=jnp.float32
    )
    key_low = jnp.einsum(
        "hqk,qhd->khd", score_grad, query_heads, preferred_element_type=jnp.float32
    ).astype(jnp.bfloat16)
    return (
        query_grad.reshape(queries.shape),
        key_low.reshape(queries.shape),
        value_grad.reshape(queries.shape),
    )


def on_device(
    layer_input,
    out_cotangent,
    mix_gain,
    mix_shift,
    query_weight,
    query_bias,
    key_weight,
    value_weight,
    value_bias,
    output_weight,
    output_bias,
    feed_gain,
    feed_shift,
    inner_weight,
    inner_bias,
    outer_weight,
    outer_bias,
):
    (
        gain_first,
        shift_first,
        query_full,
        bias_query,
        key_full,
        value_full,
        bias_value,
        output_full,
        bias_output,
        gain_second,
        shift_second,
        inner_full,
        bias_inner,
        outer_full,
        bias_outer,
    ) = (
        lax.all_gather(mix_gain, "dp", axis=0, tiled=True),
        lax.all_gather(mix_shift, "dp", axis=0, tiled=True),
        lax.all_gather(query_weight, "dp", axis=0, tiled=True),
        lax.all_gather(query_bias, "dp", axis=0, tiled=True),
        lax.all_gather(key_weight, "dp", axis=0, tiled=True),
        lax.all_gather(value_weight, "dp", axis=0, tiled=True),
        lax.all_gather(value_bias, "dp", axis=0, tiled=True),
        lax.all_gather(output_weight, "dp", axis=0, tiled=True),
        lax.all_gather(output_bias, "dp", axis=0, tiled=True),
        lax.all_gather(feed_gain, "dp", axis=0, tiled=True),
        lax.all_gather(feed_shift, "dp", axis=0, tiled=True),
        lax.all_gather(inner_weight, "dp", axis=0, tiled=True),
        lax.all_gather(inner_bias, "dp", axis=0, tiled=True),
        lax.all_gather(outer_weight, "dp", axis=0, tiled=True),
        lax.all_gather(outer_bias, "dp", axis=0, tiled=True),
    )
    clip_count = layer_input.shape[0]
    feature_count = layer_input.shape[2]
    normed_one, rstd_one, lowered_one = layer_norm(layer_input, gain_first, shift_first)
    gathered_one = lax.all_gather(lowered_one, "tensor", axis=1, tiled=True)
    frames = gathered_one.shape[1]
    flat_one = gathered_one.reshape(clip_count * frames, feature_count)
    vector_query = bias_query.astype(jnp.float32).T.reshape(-1)
    vector_value = bias_value.astype(jnp.float32).T.reshape(-1)
    vector_inner = bias_inner.astype(jnp.float32).T.reshape(-1)
    width = query_full.shape[1]
    queries = (matmul(flat_one, query_full) + vector_query).astype(jnp.bfloat16)
    key_rows = matmul(flat_one, key_full).astype(jnp.bfloat16)
    values = (matmul(flat_one, value_full) + vector_value).astype(jnp.bfloat16)
    clip_queries = queries.reshape(clip_count, frames, width)
    clip_keys = key_rows.reshape(clip_count, frames, width)
    clip_values = values.reshape(clip_count, frames, width)
    context, log_total = lax.map(attend, (clip_queries, clip_keys, clip_values))
    flat_context = context.reshape(clip_count * frames, width)
    attn_partial = matmul(flat_context, output_full.T).reshape(clip_count, frames, feature_count)
    attn_share = lax.psum_scatter(
        attn_partial.astype(jnp.bfloat16), "tensor", scatter_dimension=1, tiled=True
    ).astype(jnp.float32)
    mixed = layer_input + attn_share + bias_output.astype(jnp.float32)
    normed_two, rstd_two, lowered_two = layer_norm(mixed, gain_second, shift_second)
    gathered_two = lax.all_gather(lowered_two, "tensor", axis=1, tiled=True)
    flat_two = gathered_two.reshape(clip_count * frames, feature_count)
    preact = matmul(flat_two, inner_full) + vector_inner
    hidden = gelu_value(preact).astype(jnp.bfloat16)
    feed_partial = matmul(hidden, outer_full.T).reshape(clip_count, frames, feature_count)
    feed_share = lax.psum_scatter(
        feed_partial.astype(jnp.bfloat16), "tensor", scatter_dimension=1, tiled=True
    ).astype(jnp.float32)
    layer_output = mixed + feed_share + bias_outer.astype(jnp.float32)
    cot_low = out_cotangent.astype(jnp.bfloat16)
    cot_all = lax.all_gather(cot_low, "tensor", axis=1, tiled=True).reshape(
        clip_count * frames, feature_count
    )
    preact_grad = matmul(cot_all, outer_full) * gelu_slope(preact)
    preact_low = preact_grad.astype(jnp.bfloat16)
    outer_grad = token_product(cot_all, hidden)
    inner_grad = token_product(flat_two, preact_low)
    inner_bias_part = jnp.sum(preact_grad, axis=0).reshape(-1, HD).T
    norm_two_part = matmul(preact_low, inner_full.T).reshape(clip_count, frames, feature_count)
    norm_two_grad = lax.psum_scatter(
        norm_two_part.astype(jnp.bfloat16), "tensor", scatter_dimension=1, tiled=True
    ).astype(jnp.float32)
    feed_gain_part = jnp.sum(norm_two_grad * normed_two, axis=(0, 1))
    feed_shift_part = jnp.sum(norm_two_grad, axis=(0, 1))
    mixed_grad = out_cotangent + norm_backward(norm_two_grad, normed_two, rstd_two, gain_second)
    outer_bias_part = jnp.sum(out_cotangent, axis=(0, 1))
    output_bias_part = jnp.sum(mixed_grad, axis=(0, 1))
    mixed_low = mixed_grad.astype(jnp.bfloat16)
    mixed_all = lax.all_gather(mixed_low, "tensor", axis=1, tiled=True).reshape(
        clip_count * frames, feature_count
    )
    output_grad = token_product(mixed_all, flat_context)
    context_grad = (
        matmul(mixed_all, output_full).astype(jnp.bfloat16).reshape(clip_count, frames, width)
    )
    query_grad, key_low, value_grad = lax.map(
        attend_back, (clip_queries, clip_keys, clip_values, context_grad, log_total)
    )
    query_grad = query_grad.reshape(clip_count * frames, width)
    key_low = key_low.reshape(clip_count * frames, width)
    value_grad = value_grad.reshape(clip_count * frames, width)
    query_low = query_grad.astype(jnp.bfloat16)
    value_low = value_grad.astype(jnp.bfloat16)
    query_grad_part = token_product(flat_one, query_low)
    key_grad_part = token_product(flat_one, key_low)
    value_grad_part = token_product(flat_one, value_low)
    query_bias_part = jnp.sum(query_grad, axis=0).reshape(-1, HD).T
    value_bias_part = jnp.sum(value_grad, axis=0).reshape(-1, HD).T
    norm_one_part = (
        matmul(query_low, query_full.T)
        + matmul(key_low, key_full.T)
        + matmul(value_low, value_full.T)
    )
    norm_one_grad = lax.psum_scatter(
        norm_one_part.reshape(clip_count, frames, feature_count).astype(jnp.bfloat16),
        "tensor",
        scatter_dimension=1,
        tiled=True,
    ).astype(jnp.float32)
    mix_gain_part = jnp.sum(norm_one_grad * normed_one, axis=(0, 1))
    mix_shift_part = jnp.sum(norm_one_grad, axis=(0, 1))
    input_grad = mixed_grad + norm_backward(norm_one_grad, normed_one, rstd_one, gain_first)
    (
        query_weight_grad,
        query_bias_grad,
        key_weight_grad,
        value_weight_grad,
        value_bias_grad,
        output_weight_grad,
        inner_weight_grad,
        inner_bias_grad,
        outer_weight_grad,
    ) = (
        lax.psum_scatter(query_grad_part, "dp", scatter_dimension=0, tiled=True),
        lax.psum_scatter(query_bias_part, "dp", scatter_dimension=0, tiled=True),
        lax.psum_scatter(key_grad_part, "dp", scatter_dimension=0, tiled=True),
        lax.psum_scatter(value_grad_part, "dp", scatter_dimension=0, tiled=True),
        lax.psum_scatter(value_bias_part, "dp", scatter_dimension=0, tiled=True),
        lax.psum_scatter(output_grad, "dp", scatter_dimension=0, tiled=True),
        lax.psum_scatter(inner_grad, "dp", scatter_dimension=0, tiled=True),
        lax.psum_scatter(inner_bias_part, "dp", scatter_dimension=0, tiled=True),
        lax.psum_scatter(outer_grad, "dp", scatter_dimension=0, tiled=True),
    )
    (
        mix_gain_grad,
        mix_shift_grad,
        output_bias_grad,
        feed_gain_grad,
        feed_shift_grad,
        outer_bias_grad,
    ) = (
        lax.psum_scatter(mix_gain_part, ("dp", "tensor"), scatter_dimension=0, tiled=True),
        lax.psum_scatter(mix_shift_part, ("dp", "tensor"), scatter_dimension=0, tiled=True),
        lax.psum_scatter(output_bias_part, ("dp", "tensor"), scatter_dimension=0, tiled=True),
        lax.psum_scatter(feed_gain_part, ("dp", "tensor"), scatter_dimension=0, tiled=True),
        lax.psum_scatter(feed_shift_part, ("dp", "tensor"), scatter_dimension=0, tiled=True),
        lax.psum_scatter(outer_bias_part, ("dp", "tensor"), scatter_dimension=0, tiled=True),
    )
    return (
        layer_output,
        input_grad,
        mix_gain_grad,
        mix_shift_grad,
        query_weight_grad,
        query_bias_grad,
        key_weight_grad,
        value_weight_grad,
        value_bias_grad,
        output_weight_grad,
        output_bias_grad,
        feed_gain_grad,
        feed_shift_grad,
        inner_weight_grad,
        inner_bias_grad,
        outer_weight_grad,
        outer_bias_grad,
    )


def solution(mesh):
    placed = (
        P("dp", "tensor", None),
        P("dp", "tensor", None),
        P("dp"),
        P("dp"),
        P("dp", "tensor"),
        P("dp", "tensor"),
        P("dp", "tensor"),
        P("dp", "tensor"),
        P("dp", "tensor"),
        P("dp", "tensor"),
        P("dp"),
        P("dp"),
        P("dp"),
        P("dp", "tensor"),
        P("dp", "tensor"),
        P("dp", "tensor"),
        P("dp"),
    )
    return jax.shard_map(
        on_device,
        mesh=mesh,
        in_specs=placed,
        out_specs=(
            P("dp", "tensor", None),
            P("dp", "tensor", None),
            P(("dp", "tensor")),
            P(("dp", "tensor")),
            P("dp", "tensor"),
            P("dp", "tensor"),
            P("dp", "tensor"),
            P("dp", "tensor"),
            P("dp", "tensor"),
            P("dp", "tensor"),
            P(("dp", "tensor")),
            P(("dp", "tensor")),
            P(("dp", "tensor")),
            P("dp", "tensor"),
            P("dp", "tensor"),
            P("dp", "tensor"),
            P(("dp", "tensor")),
        ),
        check_vma=False,
    )
```

profile of v0, /device:TPU:0, one launch (start us, length us, event | category | flops | bytes accessed | tf_op | source)
XLA Modules:
  0.0 955.9 jit_solution(9160846206304437627)
XLA Ops:
  8.1 1.3 reduce_sum.173
  9.4 1.4 multiply_reduce_fusion.3
  10.8 1.3 fusion.107
  12.8 0.8 dynamic-update-slice.3
  13.7 0.8 dynamic-update-slice.4
  17.8 38.8 %all-reduce.17 = (bf16[768]{0:T(1024)(128)(2,1)S(1)}, bf16[768]{0:T(1024)(128)(2,1)S(1)}, bf16[768]{0:T(1024)(128)(2,1)S(1)}, bf16[768]{0:T(1024)(128)(2,1)S(1)}...) all-reduce(bf16[768]{0:T(1024)(128)(2,1)S(1)} %dynamic-update-slice., ...), channel_id=1, replica_groups=mesh['dp'=8,'tensor'=4] {'dp'}, use_global_device_ids=true, to_apply=%add.1 | all-reduce | flops 4608 | bytes 18432
  56.6 2.1 add_convert_fusion.2
  58.8 16.6 %all-gather.1 = bf16[8,8,3]{1,2,0:T(4,128)(2,1)S(1)} all-gather(bf16[1,8,3]{1,2,0:T(4,128)(2,1)S(1)} %bitcast.145), channel_id=1, replica_groups=mesh['dp'=8,'tensor'=4] {'dp'}, dimensions={0}, use_global_device_ids=true | all-gather | bytes 432 | tf_op jit(solution)/shard_map/all_gather | solution.py:146
  75.6 17.9 %all-gather = bf16[8,8,3]{1,2,0:T(4,128)(2,1)S(1)} all-gather(bf16[1,8,3]{1,2,0:T(4,128)(2,1)S(1)} %bitcast.146), channel_id=1, replica_groups=mesh['dp'=8,'tensor'=4] {'dp'}, dimensions={0}, use_global_device_ids=true | all-gather | bytes 432 | tf_op jit(solution)/shard_map/all_gather | solution.py:149
  93.7 31.1 %all_gather.62 = bf16[768,192]{1,0:T(8,128)(2,1)S(1)} all-gather(bf16[96,192]{1,0:T(8,128)(2,1)S(1)} %copy-done.22), channel_id=1, replica_groups=mesh['dp'=8,'tensor'=4] {'dp'}, dimensions={0}, use_global_device_ids=true | all-gather | bytes 331776 | tf_op jit(solution)/shard_map/all_gather | solution.py:145
  124.8 31.1 %all_gather.64 = bf16[768,192]{1,0:T(8,128)(2,1)S(1)} all-gather(bf16[96,192]{1,0:T(8,128)(2,1)S(1)} %copy-done.23), channel_id=1, replica_groups=mesh['dp'=8,'tensor'=4] {'dp'}, dimensions={0}, use_global_device_ids=true | all-gather | bytes 331776 | tf_op jit(solution)/shard_map/all_gather | solution.py:147
  155.9 31.1 %all_gather.60 = bf16[768,192]{1,0:T(8,128)(2,1)S(1)} all-gather(bf16[96,192]{1,0:T(8,128)(2,1)S(1)} %copy-done.24), channel_id=1, replica_groups=mesh['dp'=8,'tensor'=4] {'dp'}, dimensions={0}, use_global_device_ids=true | all-gather | bytes 331776 | tf_op jit(solution)/shard_map/all_gather | solution.py:148
  187.0 31.0 %all_gather.65 = bf16[768,192]{1,0:T(8,128)(2,1)S(1)} all-gather(bf16[96,192]{1,0:T(8,128)(2,1)S(1)} %copy-done.25), channel_id=1, replica_groups=mesh['dp'=8,'tensor'=4] {'dp'}, dimensions={0}, use_global_device_ids=true | all-gather | bytes 331776 | tf_op jit(solution)/shard_map/all_gather | solution.py:150
  217.9 2.2 fusion.58
  220.2 2.2 fusion.64
  222.4 1.9 multiply_reduce_fusion.1
  224.3 2.1 exponential_reduce_fusion
  227.6 1.5 copy-done
  229.0 2.2 convolution_convert_fusion.3
  232.0 1.8 fusion.45
  236.3 23.1 %reduce-scatter.16.cloned.1.call-done = bf16[1,256,768]{2,1,0:T(8,128)(2,1)} async-done(((bf16[1,1024,768]{2,1,0:T(8,128)(2,1)}), bf16[1,256,768]{2,1,0:T(8,128)(2,1)}) %reduce-scatter.16.cloned.1.call-update) | async-done | bytes 393232 | tf_op jit(solution)/shard_map/reduce_scatter | solution.py:178
  259.4 1.2 fusion.103
  261.7 1.6 add_convert_fusion.1
  264.0 2.9 fusion.106
  267.0 26.2 %all_gather.71 = bf16[64,12]{1,0:T(8,128)(2,1)S(1)} all-gather(bf16[8,12]{1,0:T(8,128)(2,1)} %param.31), channel_id=1, replica_groups=mesh['dp'=8,'tensor'=4] {'dp'}, dimensions={0}, use_global_device_ids=true | all-gather | bytes 1728 | tf_op jit(solution)/shard_map/all_gather | solution.py:155
  293.8 1.4 copy.60
  295.2 1.4 reshape.253
  296.6 5.5 multiply_convert_fusion.1
  302.1 37.3 %all-gather.15.cloned.1.call-done = bf16[768,768]{1,0:T(8,128)(2,1)} async-done(((bf16[96,768]{1,0:T(8,128)(2,1)}), bf16[768,768]{1,0:T(8,128)(2,1)}) %all-gather.15.cloned.1.call-update) | async-done | bytes 1179664 | tf_op jit(solution)/shard_map/all_gather | solution.py:156
  339.4 20.3 %all-gather.17.cloned.1.call-done = bf16[1,1024,768]{2,1,0:T(8,128)(2,1)} async-done(((bf16[1,256,768]{2,1,0:T(8,128)(2,1)}), bf16[1,1024,768]{2,1,0:T(8,128)(2,1)}) %all-gather.17.cloned.1.call-update) | async-done | bytes 1572880 | tf_op jit(solution)/shard_map/all_gather | solution.py:193
  359.7 5.5 fusion.110
  365.2 1.2 copy-done.34
  366.4 2.6 fusion.47
  369.0 4.4 fusion.46
  373.4 1.3 convert_element_type.153
  374.7 22.6 %reduce-scatter.20.cloned.1.call-done = bf16[1,256,768]{2,1,0:T(8,128)(2,1)} async-done(((bf16[1,1024,768]{2,1,0:T(8,128)(2,1)}), bf16[1,256,768]{2,1,0:T(8,128)(2,1)}) %reduce-scatter.20.cloned.1.call-update) | async-done | bytes 393232 | tf_op jit(solution)/shard_map/reduce_scatter | solution.py:202
  397.3 2.0 fusion.89
  399.9 28.0 %reduce-scatter.18.cloned.1.call-done = bf16[1,256,768]{2,1,0:T(8,128)(2,1)} async-done(((bf16[1,1024,768]{2,1,0:T(8,128)(2,1)}), bf16[1,256,768]{2,1,0:T(8,128)(2,1)}) %reduce-scatter.18.cloned.1.call-update) | async-done | bytes 393232 | tf_op jit(solution)/shard_map/reduce_scatter | solution.py:188
  427.9 3.3 fusion.101
  431.2 0.9 copy-done.3
  433.0 19.6 %all-gather.19.cloned.1.call-done = bf16[1,1024,768]{2,1,0:T(8,128)(2,1)} async-done(((bf16[1,256,768]{2,1,0:T(8,128)(2,1)}), bf16[1,1024,768]{2,1,0:T(8,128)(2,1)}) %all-gather.19.cloned.1.call-update) | async-done | bytes 1572880 | tf_op jit(solution)/shard_map/all_gather | solution.py:211
  452.5 2.1 fusion.61
  454.6 7.5 fusion.104
  462.2 6.3 fusion.111
  468.5 19.8 %fusion.70 = bf16[3,64,1024]{2,1,0:T(8,128)(2,1)} fusion(bf16[1024,3,64]{0,2,1:T(8,128)(2,1)S(1)} %bitcast.135, f32[3,1024,1024]{1,2,0:T(8,128)} %fusion.111, f32[3,1024,1024]{1,2,0:T(8,128)} %copy-done, f32[3,1024]{1,0:T(4,128)S(1)} %log_add_fusion), kind=kOutput, calls=%fused_computation.61 | convolution fusion | flops 431165440 | bytes 25964544 | tf_op jit(solution)/shard_map/while/body/eval_jaxpr/hqk,qhd->khd/dot_general | solution.py:97
  488.3 20.0 %fusion.105 = (f32[3,64]{1,0:T(4,128)}, bf16[1024,3,64]{0,2,1:T(8,128)(2,1)}) fusion(bf16[1024,3,64]{0,2,1:T(8,128)(2,1)S(1)} %bitcast.133, f32[3,1024,1024]{1,2,0:T(8,128)} %fusion.111, f32[3,1024,1024]{1,2,0:T(8,128)} %copy-done, f32[3,1024]{1,0:T(4,128)S(1)} %log_add_fusion), kind=kOutput, calls=%fused_computation.118 | convolution fusion | flops 431361856 | bytes 25965312 | tf_op jit(solution)/shard_map/while/body/eval_jaxpr/hqk,khd->qhd/dot_general | solution.py:94
  508.3 1.7 fusion.113
  510.7 1.9 fusion.48
  512.6 4.7 fusion.29
  517.4 4.8 convolution_bitcast_fusion
  522.3 3.1 copy.76
  525.7 2.9 fusion.23
  528.7 1.6 fusion.33
  530.3 1.6 fusion.35
  533.5 1.5 fusion.37
  535.0 37.5 %all-reduce.16 = (f32[64,3]{0,1:T(4,128)S(1)}, f32[64,3]{0,1:T(4,128)S(1)}, f32[64,12]{0,1:T(8,128)S(1)}) all-reduce(f32[64,3]{0,1:T(4,128)} %bitcast.144, f32[64,3]{0,1:T(4,128)} %bitcast.143, f32[64,12]{0,1:T(8,128)S(1)} %bitcast.140), channel_id=9, replica_groups=mesh['dp'=8,'tensor'=4] {'dp'}, use_global_device_ids=true, to_apply=%region_21.22.clone | all-reduce | flops 1152 | bytes 9216
  574.6 1.4 fusion.90
  576.0 37.7 %all-reduce.15 = (f32[768]{0:T(1024)S(1)}, f32[768]{0:T(1024)S(1)}, f32[768]{0:T(1024)S(1)}, f32[768]{0:T(1024)S(1)}, f32[768]{0:T(1024)S(1)}, /*index=5*/f32[768]{0:T(1024)S(1)}) all-reduce(f32[768]{0:T(1024)S(1)} %get-tuple-element.132, f32[768]{0:T(1024)S(1)} %get-tuple-element.137, ...), channel_id=6, replica_groups=mesh['dp'=8,'tensor'=4] {'dp','tensor'}, use_global_device_ids=true, to_apply=%region_16.17.clone | all-reduce | flops 4608 | bytes 36864
  617.2 2.2 fusion.83
  619.4 66.7 %reduce-scatter.34.cloned.1.call-done = f32[96,768]{1,0:T(8,128)} async-done(((f32[768,768]{1,0:T(8,128)}), f32[96,768]{1,0:T(8,128)}) %reduce-scatter.34.cloned.1.call-update) | async-done | bytes 294928
  686.1 65.4 %reduce-scatter.30.cloned.1.call-done = f32[96,192]{1,0:T(8,128)} async-done(((f32[768,192]{1,0:T(8,128)}), f32[96,192]{1,0:T(8,128)}) %reduce-scatter.30.cloned.1.call-update) | async-done | bytes 73744 | tf_op jit(solution)/shard_map/reduce_scatter | solution.py:261
  751.5 65.8 %reduce-scatter.28.cloned.1.call-done = f32[96,192]{1,0:T(8,128)} async-done(((f32[768,192]{1,0:T(8,128)}), f32[96,192]{1,0:T(8,128)}) %reduce-scatter.28.cloned.1.call-update) | async-done | bytes 73744 | tf_op jit(solution)/shard_map/reduce_scatter | solution.py:259
  817.3 65.4 %reduce-scatter.26.cloned.1.call-done = f32[96,192]{1,0:T(8,128)} async-done(((f32[768,192]{1,0:T(8,128)}), f32[96,192]{1,0:T(8,128)}) %reduce-scatter.26.cloned.1.call-update) | async-done | bytes 73744 | tf_op jit(solution)/shard_map/reduce_scatter | solution.py:258
  882.7 65.8 %reduce-scatter.24.cloned.1.call-done = f32[96,192]{1,0:T(8,128)} async-done(((f32[768,192]{1,0:T(8,128)}), f32[96,192]{1,0:T(8,128)}) %reduce-scatter.24.cloned.1.call-update) | async-done | bytes 73744 | tf_op jit(solution)/shard_map/reduce_scatter | solution.py:256
  (149 shorter events, 19.7 us)
Async XLA Ops:
  8.0 50.8 %copy-start.31 = (bf16[8,3]{0,1:T(4,128)(2,1)S(1)}, bf16[8,3]{0,1:T(4,128)(2,1)}, u32[]{:S(2)}) copy-start(bf16[8,3]{0,1:T(4,128)(2,1)} %param.22) | copy-start | bytes 148
  8.0 67.6 %copy-start.32 = (bf16[8,3]{0,1:T(4,128)(2,1)S(1)}, bf16[8,3]{0,1:T(4,128)(2,1)}, u32[]{:S(2)}) copy-start(bf16[8,3]{0,1:T(4,128)(2,1)} %param.25) | copy-start | bytes 148
  8.0 85.7 %copy-start.22 = (bf16[96,192]{1,0:T(8,128)(2,1)S(1)}, bf16[96,192]{1,0:T(8,128)(2,1)}, u32[]{:S(2)}) copy-start(bf16[96,192]{1,0:T(8,128)(2,1)} %param.21) | copy-start | bytes 110596
  8.1 116.8 %copy-start.23 = (bf16[96,192]{1,0:T(8,128)(2,1)S(1)}, bf16[96,192]{1,0:T(8,128)(2,1)}, u32[]{:S(2)}) copy-start(bf16[96,192]{1,0:T(8,128)(2,1)} %param.23) | copy-start | bytes 110596
  8.1 147.8 %copy-start.24 = (bf16[96,192]{1,0:T(8,128)(2,1)S(1)}, bf16[96,192]{1,0:T(8,128)(2,1)}, u32[]{:S(2)}) copy-start(bf16[96,192]{1,0:T(8,128)(2,1)} %param.24) | copy-start | bytes 110596
  8.1 178.9 %copy-start.25 = (bf16[96,192]{1,0:T(8,128)(2,1)S(1)}, bf16[96,192]{1,0:T(8,128)(2,1)}, u32[]{:S(2)}) copy-start(bf16[96,192]{1,0:T(8,128)(2,1)} %param.26) | copy-start | bytes 110596
  8.1 209.9 %all-gather.9.cloned.1.call-start = ((), (), s32[]{:S(2)}) async-start(), calls=%async_computation.10 | async-start | bytes 1966080 | tf_op jit(solution)/shard_map/all_gather | solution.py:162
  9.4 49.4 %copy-start.26 = (f32[256]{0:T(256)}, f32[256]{0:T(256)S(1)}, u32[]{:S(2)}) copy-start(f32[256]{0:T(256)S(1)} %broadcast_multiply_fusion.5) | copy-start | bytes 3076
  10.8 48.0 %copy-start.29 = (f32[256]{0:T(256)}, f32[256]{0:T(256)S(1)}, u32[]{:S(2)}) copy-start(f32[256]{0:T(256)S(1)} %add_rsqrt_fusion.1) | copy-start | bytes 3076
  56.6 68.2 %copy-start.20 = (f32[768]{0:T(1024)}, f32[768]{0:T(1024)S(1)}, u32[]{:S(2)}) copy-start(f32[768]{0:T(1024)S(1)} %convert_element_type.132) | copy-start | bytes 9220
  58.8 200.6 %reduce-scatter.16.cloned.1.call-start = ((), (), s32[]{:S(2)}) async-start(), calls=%async_computation.11 | async-start | bytes 1966080 | tf_op jit(solution)/shard_map/reduce_scatter | solution.py:178
  124.8 99.5 %copy-start.12 = (bf16[768,192]{1,0:T(8,128)(2,1)}, bf16[768,192]{1,0:T(8,128)(2,1)S(1)}, u32[]{:S(2)}) copy-start(bf16[768,192]{1,0:T(8,128)(2,1)S(1)} %all_gather.62) | copy-start | bytes 884740
  155.9 68.4 %copy-start.10 = (bf16[768,192]{1,0:T(8,128)(2,1)}, bf16[768,192]{1,0:T(8,128)(2,1)S(1)}, u32[]{:S(2)}) copy-start(bf16[768,192]{1,0:T(8,128)(2,1)S(1)} %all_gather.64) | copy-start | bytes 884740
  187.0 39.4 %copy-start.7 = (bf16[768,192]{1,0:T(8,128)(2,1)}, bf16[768,192]{1,0:T(8,128)(2,1)S(1)}, u32[]{:S(2)}) copy-start(bf16[768,192]{1,0:T(8,128)(2,1)S(1)} %all_gather.60) | copy-start | bytes 884740
  217.9 13.4 %copy-start.9 = (bf16[768,192]{1,0:T(8,128)(2,1)}, bf16[768,192]{1,0:T(8,128)(2,1)S(1)}, u32[]{:S(2)}) copy-start(bf16[768,192]{1,0:T(8,128)(2,1)S(1)} %all_gather.65) | copy-start | bytes 884740
  220.2 4.1 copy-start.14
  222.4 1.9 copy-start.16
  224.3 4.7 copy-start
  224.3 2.6 copy-start.1
  231.3 0.7 copy-start.5
  231.3 28.1 %copy-start.2 = (f32[1,256,768]{2,1,0:T(8,128)S(1)}, f32[1,256,768]{2,1,0:T(8,128)}, u32[]{:S(2)}) copy-start(f32[1,256,768]{2,1,0:T(8,128)} %param.17) | copy-start | bytes 2359300
  233.9 62.7 %all-gather.13.cloned.1.call-start = ((), (), s32[]{:S(2)}) async-start(), calls=%async_computation.13 | async-start | bytes 1327104 | tf_op jit(solution)/shard_map/all_gather | solution.py:154
  234.5 62.1 %all-gather.11.cloned.1.call-start = ((), (), s32[]{:S(2)}) async-start(), calls=%async_computation.12 | async-start | bytes 1966080 | tf_op jit(solution)/shard_map/all_gather | solution.py:183
  260.6 0.6 copy-start.28
  261.2 0.6 copy-start.30
  263.4 76.0 %all-gather.15.cloned.1.call-start = ((), (), s32[]{:S(2)}) async-start(), calls=%async_computation.14 | async-start | bytes 1327104 | tf_op jit(solution)/shard_map/all_gather | solution.py:156
  264.0 95.7 %all-gather.17.cloned.1.call-start = ((), (), s32[]{:S(2)}) async-start(), calls=%async_computation.16 | async-start | bytes 1966080 | tf_op jit(solution)/shard_map/all_gather | solution.py:193
  266.9 130.4 %reduce-scatter.20.cloned.1.call-start = ((), (), s32[]{:S(2)}) async-start(), calls=%async_computation.17 | async-start | bytes 1966080 | tf_op jit(solution)/shard_map/reduce_scatter | solution.py:202
  359.7 6.7 copy-start.33
  365.2 1.2 copy-start.34
  369.0 59.0 %reduce-scatter.18.cloned.1.call-start = ((), (), s32[]{:S(2)}) async-start(), calls=%async_computation.15 | async-start | bytes 1966080 | tf_op jit(solution)/shard_map/reduce_scatter | solution.py:188
  373.4 79.1 %all-gather.19.cloned.1.call-start = ((), (), s32[]{:S(2)}) async-start(), calls=%async_computation.18 | async-start | bytes 1966080 | tf_op jit(solution)/shard_map/all_gather | solution.py:211
  431.2 0.9 copy-start.3
  432.9 141.7 %reduce-scatter.22.cloned.1.call-start = ((), (), s32[]{:S(2)}) async-start(), calls=%async_computation.19 | async-start | bytes 1966080 | tf_op jit(solution)/shard_map/reduce_scatter | solution.py:236
  462.2 6.3 copy-start.17
  468.5 19.8 %copy-start.15 = (bf16[1024,192]{0,1:T(8,128)(2,1)S(1)}, bf16[1024,192]{0,1:T(8,128)(2,1)}, u32[]{:S(2)}) copy-start(bf16[1024,192]{0,1:T(8,128)(2,1)} %copy-done.14) | copy-start | bytes 1179652
  488.3 20.0 %copy-start.11 = (bf16[768,192]{1,0:T(8,128)(2,1)S(1)}, bf16[768,192]{1,0:T(8,128)(2,1)}, u32[]{:S(2)}) copy-start(bf16[768,192]{1,0:T(8,128)(2,1)} %copy-done.10) | copy-start | bytes 884740
  508.3 1.7 copy-start.13
  508.3 1.7 copy-start.18
  508.3 2.4 copy-start.8
  512.6 106.8 %reduce-scatter.32.cloned.1.call-start = ((), (), s32[]{:S(2)}) async-start(), calls=%async_computation.24 | async-start | bytes 2654208 | tf_op jit(solution)/shard_map/reduce_scatter | solution.py:262
  517.4 168.7 %reduce-scatter.34.cloned.1.call-start = ((), (), s32[]{:S(2)}) async-start(), calls=%async_computation.25 | async-start | bytes 2654208
  522.3 3.4 copy-start.6
  525.4 226.1 %reduce-scatter.30.cloned.1.call-start = ((), (), s32[]{:S(2)}) async-start(), calls=%async_computation.23 | async-start | bytes 884736 | tf_op jit(solution)/shard_map/reduce_scatter | solution.py:261
  528.6 1.7 copy-start.19
  528.6 288.7 %reduce-scatter.28.cloned.1.call-start = ((), (), s32[]{:S(2)}) async-start(), calls=%async_computation.22 | async-start | bytes 884736 | tf_op jit(solution)/shard_map/reduce_scatter | solution.py:259
  530.2 44.3 %copy-start.21 = (f32[768]{0:T(1024)S(1)}, f32[768]{0:T(1024)}, u32[]{:S(2)}) copy-start(f32[768]{0:T(1024)} %copy-done.20) | copy-start | bytes 9220
  530.2 44.3 %copy-start.27 = (f32[256]{0:T(256)S(1)}, f32[256]{0:T(256)}, u32[]{:S(2)}) copy-start(f32[256]{0:T(256)} %copy-done.26) | copy-start | bytes 3076
  530.3 352.4 %reduce-scatter.26.cloned.1.call-start = ((), (), s32[]{:S(2)}) async-start(), calls=%async_computation.21 | async-start | bytes 884736 | tf_op jit(solution)/shard_map/reduce_scatter | solution.py:258
  531.9 85.3 %copy-start.4 = (f32[1,256,768]{2,1,0:T(8,128)S(1)}, f32[1,256,768]{2,1,0:T(8,128)}, u32[]{:S(2)}) copy-start(f32[1,256,768]{2,1,0:T(8,128)} %copy-done.3) | copy-start | bytes 2359300
  531.9 416.6 %reduce-scatter.24.cloned.1.call-start = ((), (), s32[]{:S(2)}) async-start(), calls=%async_computation.20 | async-start | bytes 884736 | tf_op jit(solution)/shard_map/reduce_scatter | solution.py:256
Sparse Core Ops, SparseCore 0:
  58.9 16.9 all-gather.8
  234.0 25.3 reduce-scatter.15
  369.1 28.1 reduce-scatter.19
  399.7 28.1 reduce-scatter.17
Sparse Core Ops, SparseCore 1:
  236.8 38.6 all-gather.12
  277.6 18.0 all-gather.10
  297.9 41.5 all-gather.14
  341.7 18.0 all-gather.16
  433.0 19.5 all-gather.18
  512.7 28.1 reduce-scatter.21
  544.7 69.3 reduce-scatter.31
  618.0 68.0 reduce-scatter.33
  689.9 61.6 reduce-scatter.29
  755.8 61.5 reduce-scatter.27
  821.1 61.5 reduce-scatter.25
  886.9 61.5 reduce-scatter.23
where the time goes:
time: 965 us; the launch traced here: 956 us
  waiting for transfers between devices  481 us (50%)
  blocking collectives  299 us (31%)
  matrix products  106 us (11%)
  other arithmetic  26.7 us (3%)
  local copies, waits for them, and re-layouts  24.5 us (3%)
  between operations  17.4 us (2%)
    unnamed x3, blocking collectives  114 us
    unnamed x17, waiting for transfers between devices  67.5 us
    reduce_scatter x1, waiting for transfers between devices, on_device(): lax.psum_scatter(query_grad_part, 'dp', scatter_dimension=0, tiled=True)  65.8 us
    reduce_scatter x1, waiting for transfers between devices, on_device(): lax.psum_scatter(value_grad_part, 'dp', scatter_dimension=0, tiled=True)  65.8 us
    reduce_scatter x1, waiting for transfers between devices, on_device(): lax.psum_scatter(output_grad, 'dp', scatter_dimension=0, tiled=True)  65.4 us
    reduce_scatter x1, waiting for transfers between devices, on_device(): lax.psum_scatter(key_grad_part, 'dp', scatter_dimension=0, tiled=True)  65.4 us
    all_gather x1, waiting for transfers between devices, on_device(): lax.all_gather(outer_weight, 'dp', axis=0, tiled=True)  37.3 us
    dot_general x12, matrix products, matmul(): return jnp.dot(left, right, preferred_element_type=jnp.float32)  31.2 us
  transfers between devices with their start and end apart: 16, of which 11 were waited for; matrix products, arithmetic and copies ran while one was open for 6% of the time, Pallas kernels for 0%

commit v1 on v0

--- a/solution.py
+++ b/solution.py
@@ -8,6 +8,28 @@
 EPS = 1e-05
 ROOT_HALF = 0.7071067811865476
 DENSITY_NORM = 0.3989422804014327
+
+
+def laid_out(blocks, dim):
+    blocks = jnp.moveaxis(blocks, 0, dim)
+    dims = blocks.shape
+    return blocks.reshape(*dims[:dim], dims[dim] * dims[dim + 1], *dims[dim + 2 :])
+
+
+def collect(x, axis, dim):
+    size = lax.axis_size(axis)
+    pairs = [(i, (i + 1) % size) for i in range(size)]
+    back = [(b, a) for a, b in pairs]
+    lower, upper = ([], [])
+    for step in range(size - 1):
+        if step % 2 == 0:
+            lower.append(lax.ppermute(lower[-1] if lower else x, axis, pairs))
+        else:
+            upper.append(lax.ppermute(upper[-1] if upper else x, axis, back))
+    parts = jnp.stack([*lower[::-1], x, *upper])
+    shift = lax.axis_index(axis) - len(lower)
+    parts = parts[(jnp.arange(size) - shift) % size]
+    return laid_out(parts, dim)
 
 
 def layer_norm(block, gain, shift):
@@ -147,7 +169,7 @@
         lax.all_gather(key_weight, "dp", axis=0, tiled=True),
         lax.all_gather(value_weight, "dp", axis=0, tiled=True),
         lax.all_gather(value_bias, "dp", axis=0, tiled=True),
-        lax.all_gather(output_weight, "dp", axis=0, tiled=True),
+        collect(output_weight, "dp", 0),
         lax.all_gather(output_bias, "dp", axis=0, tiled=True),
         lax.all_gather(feed_gain, "dp", axis=0, tiled=True),
         lax.all_gather(feed_shift, "dp", axis=0, tiled=True),

time: 965 us -> 950 us (0.984)
  blocking collectives: 299 us -> 265 us
  starting transfers between devices: 1.36 us -> 16.8 us
    all_gather x1 -> x0, blocking collectives: 31 us -> none  [on_device(): lax.all_gather(output_weight, 'dp', axis=0, tiled=True)]
    ppermute x0 -> x7, starting transfers between devices: none -> 15.9 us  [the longest x3 10.9 us: collect(): upper.append(lax.ppermute(upper[-1] if upper else x, axis, back))]
    unnamed x94 -> x101, local copies, waits for them, and re-layouts: 20.7 us -> 20.7 us
  transfers between devices with their start and end apart: 16 -> 23, of which waited for: 11 -> 14; matrix products, arithmetic and copies ran while one was open for 6% -> 7% of each run, Pallas kernels for 0% -> 0%
where the time goes in v1:
time: 950 us; the launch traced here: 945 us
  waiting for transfers between devices  488 us (51%)
  blocking collectives  265 us (28%)
  matrix products  106 us (11%)
  other arithmetic  26.7 us (3%)
  local copies, waits for them, and re-layouts  25.1 us (3%)
  between operations  17.5 us (2%)
  starting transfers between devices  16.8 us (2%)
    unnamed x3, blocking collectives  110 us
    unnamed x17, waiting for transfers between devices  67.4 us
    reduce_scatter x1, waiting for transfers between devices, on_device(): lax.psum_scatter(value_grad_part, 'dp', scatter_dimension=0, tiled=True)  65.8 us
    reduce_scatter x1, waiting for transfers between devices, on_device(): lax.psum_scatter(query_grad_part, 'dp', scatter_dimension=0, tiled=True)  65.8 us
    reduce_scatter x1, waiting for transfers between devices, on_device(): lax.psum_scatter(output_grad, 'dp', scatter_dimension=0, tiled=True)  65.4 us
    reduce_scatter x1, waiting for transfers between devices, on_device(): lax.psum_scatter(key_grad_part, 'dp', scatter_dimension=0, tiled=True)  65.4 us
    all_gather x1, waiting for transfers between devices, on_device(): lax.all_gather(outer_weight, 'dp', axis=0, tiled=True)  36.6 us
    dot_general x12, matrix products, matmul(): return jnp.dot(left, right, preferred_element_type=jnp.float32)  31.3 us
  transfers between devices with their start and end apart: 23, of which 14 were waited for; matrix products, arithmetic and copies ran while one was open for 7% of the time, Pallas kernels for 0%

profile of v1, /device:TPU:0, one launch (start us, length us, event | category | flops | bytes accessed | tf_op | source)
XLA Modules:
  0.0 945.4 jit_solution(1673623032962022)
XLA Ops:
  8.1 3.0 collective-permute-start
  11.1 3.1 collective-permute-start.4
  15.5 1.4 multiply_reduce_fusion.3
  16.9 1.3 fusion.109
  23.9 34.8 %all-reduce.17 = (bf16[768]{0:T(1024)(128)(2,1)S(1)}, bf16[768]{0:T(1024)(128)(2,1)S(1)}, bf16[768]{0:T(1024)(128)(2,1)S(1)}, bf16[768]{0:T(1024)(128)(2,1)S(1)}...) all-reduce(bf16[768]{0:T(1024)(128)(2,1)S(1)} %dynamic-update-slice., ...), channel_id=1, replica_groups=mesh['dp'=8,'tensor'=4] {'dp'}, use_global_device_ids=true, to_apply=%add.1 | all-reduce | flops 4608 | bytes 18432
  58.7 2.1 add_convert_fusion.2
  60.9 16.6 %all-gather.1 = bf16[8,8,3]{1,2,0:T(4,128)(2,1)S(1)} all-gather(bf16[1,8,3]{1,2,0:T(4,128)(2,1)S(1)} %bitcast.166), channel_id=1, replica_groups=mesh['dp'=8,'tensor'=4] {'dp'}, dimensions={0}, use_global_device_ids=true | all-gather | bytes 432 | tf_op jit(solution)/shard_map/all_gather | solution.py:168
  77.5 17.9 %all-gather = bf16[8,8,3]{1,2,0:T(4,128)(2,1)S(1)} all-gather(bf16[1,8,3]{1,2,0:T(4,128)(2,1)S(1)} %bitcast.167), channel_id=1, replica_groups=mesh['dp'=8,'tensor'=4] {'dp'}, dimensions={0}, use_global_device_ids=true | all-gather | bytes 432 | tf_op jit(solution)/shard_map/all_gather | solution.py:171
  95.4 31.1 %all_gather.59 = bf16[768,192]{1,0:T(8,128)(2,1)S(1)} all-gather(bf16[96,192]{1,0:T(8,128)(2,1)S(1)} %copy-done.22), channel_id=1, replica_groups=mesh['dp'=8,'tensor'=4] {'dp'}, dimensions={0}, use_global_device_ids=true | all-gather | bytes 331776 | tf_op jit(solution)/shard_map/all_gather | solution.py:167
  126.5 31.1 %all_gather.61 = bf16[768,192]{1,0:T(8,128)(2,1)S(1)} all-gather(bf16[96,192]{1,0:T(8,128)(2,1)S(1)} %copy-done.23), channel_id=1, replica_groups=mesh['dp'=8,'tensor'=4] {'dp'}, dimensions={0}, use_global_device_ids=true | all-gather | bytes 331776 | tf_op jit(solution)/shard_map/all_gather | solution.py:169
  157.7 31.0 %all_gather.57 = bf16[768,192]{1,0:T(8,128)(2,1)S(1)} all-gather(bf16[96,192]{1,0:T(8,128)(2,1)S(1)} %copy-done.24), channel_id=1, replica_groups=mesh['dp'=8,'tensor'=4] {'dp'}, dimensions={0}, use_global_device_ids=true | all-gather | bytes 331776 | tf_op jit(solution)/shard_map/all_gather | solution.py:170
  188.7 1.9 collective-permute-start.2
  190.7 2.8 collective-permute-start.5
  193.5 2.0 collective-permute-done.2
  195.9 5.0 collective-permute-start.6
  200.9 1.4 collective-permute-done.3
  203.2 2.2 fusion.58
  205.4 2.2 fusion.64
  207.7 1.9 multiply_reduce_fusion.1
  209.6 2.1 exponential_reduce_fusion
  212.8 1.5 copy-done
  214.3 2.2 convolution_convert_fusion.3
  217.3 1.9 fusion.45
  221.6 28.0 %reduce-scatter.16.cloned.1.call-done = bf16[1,256,768]{2,1,0:T(8,128)(2,1)} async-done(((bf16[1,1024,768]{2,1,0:T(8,128)(2,1)}), bf16[1,256,768]{2,1,0:T(8,128)(2,1)}) %reduce-scatter.16.cloned.1.call-update) | async-done | bytes 393232 | tf_op jit(solution)/shard_map/reduce_scatter | solution.py:200
  251.9 1.6 add_convert_fusion.1
  254.2 2.9 fusion.108
  257.1 26.7 %all_gather.67 = bf16[64,12]{1,0:T(8,128)(2,1)S(1)} all-gather(bf16[8,12]{1,0:T(8,128)(2,1)} %param.31), channel_id=1, replica_groups=mesh['dp'=8,'tensor'=4] {'dp'}, dimensions={0}, use_global_device_ids=true | all-gather | bytes 1728 | tf_op jit(solution)/shard_map/all_gather | solution.py:177
  284.5 1.4 copy.60
  285.9 1.4 reshape.306
  287.3 5.5 multiply_convert_fusion.1
  292.8 36.6 %all-gather.15.cloned.1.call-done = bf16[768,768]{1,0:T(8,128)(2,1)} async-done(((bf16[96,768]{1,0:T(8,128)(2,1)}), bf16[768,768]{1,0:T(8,128)(2,1)}) %all-gather.15.cloned.1.call-update) | async-done | bytes 1179664 | tf_op jit(solution)/shard_map/all_gather | solution.py:178
  329.4 20.3 %all-gather.17.cloned.1.call-done = bf16[1,1024,768]{2,1,0:T(8,128)(2,1)} async-done(((bf16[1,256,768]{2,1,0:T(8,128)(2,1)}), bf16[1,1024,768]{2,1,0:T(8,128)(2,1)}) %all-gather.17.cloned.1.call-update) | async-done | bytes 1572880 | tf_op jit(solution)/shard_map/all_gather | solution.py:215
  349.6 5.5 fusion.112
  356.3 2.6 fusion.47
  358.9 4.4 fusion.46
  363.4 1.3 convert_element_type.152
  364.6 22.6 %reduce-scatter.20.cloned.1.call-done = bf16[1,256,768]{2,1,0:T(8,128)(2,1)} async-done(((bf16[1,1024,768]{2,1,0:T(8,128)(2,1)}), bf16[1,256,768]{2,1,0:T(8,128)(2,1)}) %reduce-scatter.20.cloned.1.call-update) | async-done | bytes 393232 | tf_op jit(solution)/shard_map/reduce_scatter | solution.py:224
  387.2 2.0 fusion.89
  389.8 28.0 %reduce-scatter.18.cloned.1.call-done = bf16[1,256,768]{2,1,0:T(8,128)(2,1)} async-done(((bf16[1,1024,768]{2,1,0:T(8,128)(2,1)}), bf16[1,256,768]{2,1,0:T(8,128)(2,1)}) %reduce-scatter.18.cloned.1.call-update) | async-done | bytes 393232 | tf_op jit(solution)/shard_map/reduce_scatter | solution.py:210
  417.8 3.3 fusion.103
  422.8 19.6 %all-gather.19.cloned.1.call-done = bf16[1,1024,768]{2,1,0:T(8,128)(2,1)} async-done(((bf16[1,256,768]{2,1,0:T(8,128)(2,1)}), bf16[1,1024,768]{2,1,0:T(8,128)(2,1)}) %all-gather.19.cloned.1.call-update) | async-done | bytes 1572880 | tf_op jit(solution)/shard_map/all_gather | solution.py:233
  442.4 2.1 fusion.61
  444.5 7.5 fusion.106
  452.1 6.3 fusion.113
  458.4 19.7 %fusion.70 = bf16[3,64,1024]{2,1,0:T(8,128)(2,1)} fusion(bf16[1024,3,64]{0,2,1:T(8,128)(2,1)S(1)} %bitcast.156, f32[3,1024,1024]{1,2,0:T(8,128)} %fusion.113, f32[3,1024,1024]{1,2,0:T(8,128)} %copy-done, f32[3,1024]{1,0:T(4,128)S(1)} %log_add_fusion), kind=kOutput, calls=%fused_computation.62 | convolution fusion | flops 431165440 | bytes 25964544 | tf_op jit(solution)/shard_map/while/body/eval_jaxpr/hqk,qhd->khd/dot_general | solution.py:119
  478.1 20.0 %fusion.107 = (f32[3,64]{1,0:T(4,128)}, bf16[1024,3,64]{0,2,1:T(8,128)(2,1)}) fusion(bf16[1024,3,64]{0,2,1:T(8,128)(2,1)S(1)} %bitcast.154, f32[3,1024,1024]{1,2,0:T(8,128)} %fusion.113, f32[3,1024,1024]{1,2,0:T(8,128)} %copy-done, f32[3,1024]{1,0:T(4,128)S(1)} %log_add_fusion), kind=kOutput, calls=%fused_computation.134 | convolution fusion | flops 431361856 | bytes 25965312 | tf_op jit(solution)/shard_map/while/body/eval_jaxpr/hqk,khd->qhd/dot_general | solution.py:116
  498.1 1.7 fusion.115
  500.5 1.9 fusion.48
  502.5 4.7 fusion.29
  507.3 4.8 convolution_bitcast_fusion
  512.1 3.1 copy.76
  515.5 2.9 fusion.23
  518.5 1.5 fusion.33
  520.1 1.6 fusion.35
  523.3 1.5 fusion.37
  524.8 37.5 %all-reduce.16 = (f32[64,3]{0,1:T(4,128)S(1)}, f32[64,3]{0,1:T(4,128)S(1)}, f32[64,12]{0,1:T(8,128)S(1)}) all-reduce(f32[64,3]{0,1:T(4,128)} %bitcast.165, f32[64,3]{0,1:T(4,128)} %bitcast.164, f32[64,12]{0,1:T(8,128)S(1)} %bitcast.161), channel_id=9, replica_groups=mesh['dp'=8,'tensor'=4] {'dp'}, use_global_device_ids=true, to_apply=%region_21.22.clone | all-reduce | flops 1152 | bytes 9216
  564.4 1.4 fusion.90
  565.8 37.9 %all-reduce.15 = (f32[768]{0:T(1024)S(1)}, f32[768]{0:T(1024)S(1)}, f32[768]{0:T(1024)S(1)}, f32[768]{0:T(1024)S(1)}, f32[768]{0:T(1024)S(1)}, /*index=5*/f32[768]{0:T(1024)S(1)}) all-reduce(f32[768]{0:T(1024)S(1)} %get-tuple-element.132, f32[768]{0:T(1024)S(1)} %get-tuple-element.137, ...), channel_id=6, replica_groups=mesh['dp'=8,'tensor'=4] {'dp','tensor'}, use_global_device_ids=true, to_apply=%region_16.17.clone | all-reduce | flops 4608 | bytes 36864
  607.3 2.2 fusion.83
  609.4 66.2 %reduce-scatter.34.cloned.1.call-done = f32[96,768]{1,0:T(8,128)} async-done(((f32[768,768]{1,0:T(8,128)}), f32[96,768]{1,0:T(8,128)}) %reduce-scatter.34.cloned.1.call-update) | async-done | bytes 294928
  675.6 65.4 %reduce-scatter.30.cloned.1.call-done = f32[96,192]{1,0:T(8,128)} async-done(((f32[768,192]{1,0:T(8,128)}), f32[96,192]{1,0:T(8,128)}) %reduce-scatter.30.cloned.1.call-update) | async-done | bytes 73744 | tf_op jit(solution)/shard_map/reduce_scatter | solution.py:283
  741.0 65.8 %reduce-scatter.28.cloned.1.call-done = f32[96,192]{1,0:T(8,128)} async-done(((f32[768,192]{1,0:T(8,128)}), f32[96,192]{1,0:T(8,128)}) %reduce-scatter.28.cloned.1.call-update) | async-done | bytes 73744 | tf_op jit(solution)/shard_map/reduce_scatter | solution.py:281
  806.9 65.4 %reduce-scatter.26.cloned.1.call-done = f32[96,192]{1,0:T(8,128)} async-done(((f32[768,192]{1,0:T(8,128)}), f32[96,192]{1,0:T(8,128)}) %reduce-scatter.26.cloned.1.call-update) | async-done | bytes 73744 | tf_op jit(solution)/shard_map/reduce_scatter | solution.py:280
  872.2 65.8 %reduce-scatter.24.cloned.1.call-done = f32[96,192]{1,0:T(8,128)} async-done(((f32[768,192]{1,0:T(8,128)}), f32[96,192]{1,0:T(8,128)}) %reduce-scatter.24.cloned.1.call-update) | async-done | bytes 73744 | tf_op jit(solution)/shard_map/reduce_scatter | solution.py:278
  (173 shorter events, 26.8 us)
Async XLA Ops:
  8.0 194.3 %copy-start.25 = (bf16[96,192]{1,0:T(8,128)(2,1)S(1)}, bf16[96,192]{1,0:T(8,128)(2,1)}, u32[]{:S(2)}) copy-start(bf16[96,192]{1,0:T(8,128)(2,1)} %param.26) | copy-start | bytes 110596
  8.0 52.8 %copy-start.31 = (bf16[8,3]{0,1:T(4,128)(2,1)S(1)}, bf16[8,3]{0,1:T(4,128)(2,1)}, u32[]{:S(2)}) copy-start(bf16[8,3]{0,1:T(4,128)(2,1)} %param.22) | copy-start | bytes 148
  8.0 69.5 %copy-start.32 = (bf16[8,3]{0,1:T(4,128)(2,1)S(1)}, bf16[8,3]{0,1:T(4,128)(2,1)}, u32[]{:S(2)}) copy-start(bf16[8,3]{0,1:T(4,128)(2,1)} %param.25) | copy-start | bytes 148
  8.1 87.4 %copy-start.22 = (bf16[96,192]{1,0:T(8,128)(2,1)S(1)}, bf16[96,192]{1,0:T(8,128)(2,1)}, u32[]{:S(2)}) copy-start(bf16[96,192]{1,0:T(8,128)(2,1)} %param.21) | copy-start | bytes 110596
  8.1 118.5 %copy-start.23 = (bf16[96,192]{1,0:T(8,128)(2,1)S(1)}, bf16[96,192]{1,0:T(8,128)(2,1)}, u32[]{:S(2)}) copy-start(bf16[96,192]{1,0:T(8,128)(2,1)} %param.23) | copy-start | bytes 110596
  8.1 149.6 %copy-start.24 = (bf16[96,192]{1,0:T(8,128)(2,1)S(1)}, bf16[96,192]{1,0:T(8,128)(2,1)}, u32[]{:S(2)}) copy-start(bf16[96,192]{1,0:T(8,128)(2,1)} %param.24) | copy-start | bytes 110596
  8.1 195.1 %all-gather.9.cloned.1.call-start = ((), (), s32[]{:S(2)}) async-start(), calls=%async_computation.10 | async-start | bytes 1966080 | tf_op jit(solution)/shard_map/all_gather | solution.py:184
  8.1 149.5 %collective-permute-start = (bf16[96,192]{1,0:T(8,128)(2,1)}, bf16[96,192]{1,0:T(8,128)(2,1)S(1)}, u32[]{:S(2)}, u32[]{:S(2)}) collective-permute-start(bf16[96,192]{1,0:T(8,128)(2,1)} %param.26), channel_id=1, source_target_pairs={{0,4},{4,8},{8,12},{12,16},{16,20},{20,24},{24,28},{28,0},{1,5},{5... | collective-permute-start | bytes 110600 | tf_op jit(solution)/shard_map/ppermute | solution.py:26
  11.1 179.6 %collective-permute-start.4 = (bf16[96,192]{1,0:T(8,128)(2,1)}, bf16[96,192]{1,0:T(8,128)(2,1)S(1)}, u32[]{:S(2)}, u32[]{:S(2)}) collective-permute-start(bf16[96,192]{1,0:T(8,128)(2,1)} %param.26), channel_id=1, source_target_pairs={{4,0},{8,4},{12,8},{16,12},{20,16},{24,20},{28,24},{0,28},{5,1},{9... | collective-permute-start | bytes 110600 | tf_op jit(solution)/shard_map/ppermute | solution.py:28
  15.5 185.4 %copy-start.26 = (f32[256]{0:T(256)}, f32[256]{0:T(256)S(1)}, u32[]{:S(2)}) copy-start(f32[256]{0:T(256)S(1)} %broadcast_multiply_fusion.5) | copy-start | bytes 3076
  16.9 184.0 %copy-start.29 = (f32[256]{0:T(256)}, f32[256]{0:T(256)S(1)}, u32[]{:S(2)}) copy-start(f32[256]{0:T(256)S(1)} %add_rsqrt_fusion.1) | copy-start | bytes 3076
  58.7 98.9 %copy-start.20 = (f32[768]{0:T(1024)}, f32[768]{0:T(1024)S(1)}, u32[]{:S(2)}) copy-start(f32[768]{0:T(1024)S(1)} %convert_element_type.131) | copy-start | bytes 9220
  60.8 188.7 %reduce-scatter.16.cloned.1.call-start = ((), (), s32[]{:S(2)}) async-start(), calls=%async_computation.11 | async-start | bytes 1966080 | tf_op jit(solution)/shard_map/reduce_scatter | solution.py:200
  126.5 81.1 %copy-start.12 = (bf16[768,192]{1,0:T(8,128)(2,1)}, bf16[768,192]{1,0:T(8,128)(2,1)S(1)}, u32[]{:S(2)}) copy-start(bf16[768,192]{1,0:T(8,128)(2,1)S(1)} %all_gather.59) | copy-start | bytes 884740
  157.6 50.1 %copy-start.10 = (bf16[768,192]{1,0:T(8,128)(2,1)}, bf16[768,192]{1,0:T(8,128)(2,1)S(1)}, u32[]{:S(2)}) copy-start(bf16[768,192]{1,0:T(8,128)(2,1)S(1)} %all_gather.61) | copy-start | bytes 884740
  157.6 31.1 %collective-permute-start.1 = (bf16[96,192]{1,0:T(8,128)(2,1)S(1)}, bf16[96,192]{1,0:T(8,128)(2,1)S(1)}, u32[]{:S(2)}, u32[]{:S(2)}) collective-permute-start(bf16[96,192]{1,0:T(8,128)(2,1)S(1)} %collective-permute-done), channel_id=1, source_target_pairs={{0,4},{4,8},{8,12},{12,16},{16,20},{20,24},{24,28},{28,0},{1,5},{5... | collective-permute-start | bytes 110600 | tf_op jit(solution)/shard_map/ppermute | solution.py:26
  188.7 23.0 %copy-start.7 = (bf16[768,192]{1,0:T(8,128)(2,1)}, bf16[768,192]{1,0:T(8,128)(2,1)S(1)}, u32[]{:S(2)}) copy-start(bf16[768,192]{1,0:T(8,128)(2,1)S(1)} %all_gather.57) | copy-start | bytes 884740
  188.7 6.8 collective-permute-start.2
  190.7 5.2 collective-permute-start.5
  195.5 6.8 collective-permute-start.3
  195.9 6.7 collective-permute-start.6
  203.2 13.4 %copy-start.9 = (bf16[8,96,192]{2,1,0:T(8,128)(2,1)}, bf16[8,96,192]{2,1,0:T(8,128)(2,1)S(1)}, u32[]{:S(2)}) copy-start(bf16[8,96,192]{2,1,0:T(8,128)(2,1)S(1)} %gather_fusion) | copy-start | bytes 884740
  205.4 4.1 copy-start.14
  207.7 1.9 copy-start.16
  209.6 4.7 copy-start
  209.6 2.6 copy-start.1
  216.5 0.8 copy-start.5
  216.5 33.0 %copy-start.2 = (f32[1,256,768]{2,1,0:T(8,128)S(1)}, f32[1,256,768]{2,1,0:T(8,128)}, u32[]{:S(2)}) copy-start(f32[1,256,768]{2,1,0:T(8,128)} %param.17) | copy-start | bytes 2359300
  219.2 68.1 %all-gather.13.cloned.1.call-start = ((), (), s32[]{:S(2)}) async-start(), calls=%async_computation.13 | async-start | bytes 1327104 | tf_op jit(solution)/shard_map/all_gather | solution.py:176
  219.8 67.5 %all-gather.11.cloned.1.call-start = ((), (), s32[]{:S(2)}) async-start(), calls=%async_computation.12 | async-start | bytes 1966080 | tf_op jit(solution)/shard_map/all_gather | solution.py:205
  250.8 0.6 copy-start.28
  251.3 0.6 copy-start.30
  253.6 75.8 %all-gather.15.cloned.1.call-start = ((), (), s32[]{:S(2)}) async-start(), calls=%async_computation.14 | async-start | bytes 1327104 | tf_op jit(solution)/shard_map/all_gather | solution.py:178
  254.1 95.5 %all-gather.17.cloned.1.call-start = ((), (), s32[]{:S(2)}) async-start(), calls=%async_computation.16 | async-start | bytes 1966080 | tf_op jit(solution)/shard_map/all_gather | solution.py:215
  257.1 130.1 %reduce-scatter.20.cloned.1.call-start = ((), (), s32[]{:S(2)}) async-start(), calls=%async_computation.17 | async-start | bytes 1966080 | tf_op jit(solution)/shard_map/reduce_scatter | solution.py:224
  349.6 6.6 copy-start.33
  355.1 1.1 copy-start.34
  358.9 58.9 %reduce-scatter.18.cloned.1.call-start = ((), (), s32[]{:S(2)}) async-start(), calls=%async_computation.15 | async-start | bytes 1966080 | tf_op jit(solution)/shard_map/reduce_scatter | solution.py:210
  363.3 79.1 %all-gather.19.cloned.1.call-start = ((), (), s32[]{:S(2)}) async-start(), calls=%async_computation.18 | async-start | bytes 1966080 | tf_op jit(solution)/shard_map/all_gather | solution.py:233
  421.1 0.9 copy-start.3
  422.8 141.6 %reduce-scatter.22.cloned.1.call-start = ((), (), s32[]{:S(2)}) async-start(), calls=%async_computation.19 | async-start | bytes 1966080 | tf_op jit(solution)/shard_map/reduce_scatter | solution.py:258
  452.1 6.3 copy-start.17
  458.4 19.7 %copy-start.15 = (bf16[1024,192]{0,1:T(8,128)(2,1)S(1)}, bf16[1024,192]{0,1:T(8,128)(2,1)}, u32[]{:S(2)}) copy-start(bf16[1024,192]{0,1:T(8,128)(2,1)} %copy-done.14) | copy-start | bytes 1179652
  478.1 20.0 %copy-start.11 = (bf16[768,192]{1,0:T(8,128)(2,1)S(1)}, bf16[768,192]{1,0:T(8,128)(2,1)}, u32[]{:S(2)}) copy-start(bf16[768,192]{1,0:T(8,128)(2,1)} %copy-done.10) | copy-start | bytes 884740
  498.1 1.7 copy-start.13
  498.1 1.7 copy-start.18
  498.1 2.4 copy-start.8
  502.4 107.0 %reduce-scatter.32.cloned.1.call-start = ((), (), s32[]{:S(2)}) async-start(), calls=%async_computation.24 | async-start | bytes 2654208 | tf_op jit(solution)/shard_map/reduce_scatter | solution.py:284
  507.3 168.4 %reduce-scatter.34.cloned.1.call-start = ((), (), s32[]{:S(2)}) async-start(), calls=%async_computation.25 | async-start | bytes 2654208
  512.1 3.4 copy-start.6
  515.3 225.8 %reduce-scatter.30.cloned.1.call-start = ((), (), s32[]{:S(2)}) async-start(), calls=%async_computation.23 | async-start | bytes 884736 | tf_op jit(solution)/shard_map/reduce_scatter | solution.py:283
  518.5 1.7 copy-start.19
  518.5 288.4 %reduce-scatter.28.cloned.1.call-start = ((), (), s32[]{:S(2)}) async-start(), calls=%async_computation.22 | async-start | bytes 884736 | tf_op jit(solution)/shard_map/reduce_scatter | solution.py:281
  520.1 44.3 %copy-start.21 = (f32[768]{0:T(1024)S(1)}, f32[768]{0:T(1024)}, u32[]{:S(2)}) copy-start(f32[768]{0:T(1024)} %copy-done.20) | copy-start | bytes 9220
  520.1 44.3 %copy-start.27 = (f32[256]{0:T(256)S(1)}, f32[256]{0:T(256)}, u32[]{:S(2)}) copy-start(f32[256]{0:T(256)} %copy-done.26) | copy-start | bytes 3076
  520.1 352.2 %reduce-scatter.26.cloned.1.call-start = ((), (), s32[]{:S(2)}) async-start(), calls=%async_computation.21 | async-start | bytes 884736 | tf_op jit(solution)/shard_map/reduce_scatter | solution.py:280
  521.7 85.5 %copy-start.4 = (f32[1,256,768]{2,1,0:T(8,128)S(1)}, f32[1,256,768]{2,1,0:T(8,128)}, u32[]{:S(2)}) copy-start(f32[1,256,768]{2,1,0:T(8,128)} %copy-done.3) | copy-start | bytes 2359300
  521.8 416.3 %reduce-scatter.24.cloned.1.call-start = ((), (), s32[]{:S(2)}) async-start(), calls=%async_computation.20 | async-start | bytes 884736 | tf_op jit(solution)/shard_map/reduce_scatter | solution.py:278
Sparse Core Ops, SparseCore 0:
  60.9 16.9 all-gather.8
  219.3 30.2 reduce-scatter.15
  359.0 28.1 reduce-scatter.19
  389.6 28.1 reduce-scatter.17
Sparse Core Ops, SparseCore 1:
  222.1 43.3 all-gather.12
  267.5 18.0 all-gather.10
  287.8 41.5 all-gather.14
  331.6 18.0 all-gather.16
  422.9 19.5 all-gather.18
  502.5 28.1 reduce-scatter.21
  534.6 68.9 reduce-scatter.31
  607.5 68.0 reduce-scatter.33
  679.4 61.6 reduce-scatter.29
  745.3 61.5 reduce-scatter.27
  810.6 61.6 reduce-scatter.25
  876.5 61.5 reduce-scatter.23
